TPU v7x, 32 devices: a whole 2x2x4 slice. The times are simulated.
32 devices in a mesh: grp: 4 (over y, core), shard: 8 (over z, x).
Axes of the slice: x: 2, y: 2, z: 4, core: 2. Of those that a mesh axis runs over, the one named last changes fastest.
Arguments:
- table: float32 [32768, 256], P('shard'), may hold values from -6 to 6
- accum: float32 [32768], P('shard'), may hold values from 0.05 to 2
- pooled_grad: bfloat16 [4, 8, 512, 256], P('grp', 'shard'), may hold values from -6 to 6
- row_ids: int32 [4, 8, 4096], P('grp', 'shard'), may hold values from 0 to 32767, as said below
- bag_ids: int32 [4, 8, 4096], P('grp', 'shard'), may hold values from 0 to 511, never falling along the last dimension, each value on 1 to 16 neighbouring positions
- touched: int32 [8, 1024], P('shard'), may hold values from 0 to 4095, as said below
Outputs:
- new_table: float32 [32768, 256], P('shard')
- new_accum: float32 [32768], P('shard')
Inputs may be any that keep to these rules, and one draw needn't show every extreme that they name: `row_ids`: every id is s * 4096 + touched[s, k] for some shard s and some k: it lies in a listed row. At most 512 lookups of one device fall on one shard s (ids in s * 4096 to (s + 1) * 4096 - 1); in every draw some device sends exactly 512 to some shard, and in each replica one shard receives 512 from every device of that replica. Each row of touched holds 1024 distinct row numbers in increasing order.
All inputs are finite; a program needn't handle non-finite values.
Results may differ from a plain program's by a relative error of at most 0.0003.
Values may be sent and summed in bfloat16 or wider, within the bound.
A program may use at most 128 MiB of HBM per device.

v0:
```python
import jax
import jax.numpy as jnp
from jax import lax
from jax.sharding import PartitionSpec as P


def expand(listed, slot_rows, slot_grads):
    count = listed.shape[0]
    block = min(128, count)
    blocks = listed.reshape(count // block, block)

    def one_block(block_rows):
        hits = (block_rows[:, None] == slot_rows[None, :]).astype(jnp.bfloat16)
        return jnp.dot(hits, slot_grads, preferred_element_type=jnp.float32)

    return lax.map(one_block, blocks).reshape(count, slot_grads.shape[1])


def adagrad(rows_now, accum_now, grads):
    accum_next = accum_now + jnp.mean(grads * grads, axis=1)
    rows_next = rows_now - 0.5 * grads / (jnp.sqrt(accum_next)[:, None] + 1e-08)
    return (rows_next, accum_next)


def body(table, accum, pooled_grad, row_ids, bag_ids, touched):
    shards = lax.axis_size("shard")
    rows_dev = table.shape[0]
    width = table.shape[1]
    samples = pooled_grad.shape[2]
    grads = pooled_grad.reshape(samples, width)
    ids = row_ids.reshape(-1)
    bags = bag_ids.reshape(-1)
    looks = ids.shape[0]
    slots_each = looks // 8
    listed = touched.reshape(-1)
    owner = ids // rows_dev
    onehot_owner = (owner[:, None] == jnp.arange(shards, dtype=jnp.int32)[None, :]).astype(
        jnp.int32
    )
    ranks = jnp.sum((jnp.cumsum(onehot_owner, axis=0) - 1) * onehot_owner, axis=1)
    slot = owner * slots_each + ranks
    lookup_rows = jnp.take(grads, bags, axis=0)
    send_grads = jnp.zeros((shards * slots_each, width), jnp.bfloat16).at[slot].set(lookup_rows)
    send_rows = jnp.full((shards * slots_each,), -1, jnp.int32).at[slot].set(ids % rows_dev)
    send_grads = send_grads.reshape(shards, slots_each, width)
    send_rows = send_rows.reshape(shards, slots_each)
    got_grads, got_rows = (
        lax.all_to_all(send_grads, "shard", split_axis=0, concat_axis=0, tiled=True),
        lax.all_to_all(send_rows, "shard", split_axis=0, concat_axis=0, tiled=True),
    )
    grad_rows = expand(listed, got_rows.reshape(-1), got_grads.reshape(-1, width))
    share = lax.psum_scatter(grad_rows, "grp", scatter_dimension=0, tiled=True)
    count = share.shape[0]
    mine = lax.dynamic_slice_in_dim(listed, lax.axis_index("grp") * count, count)
    rows_next, accum_next = adagrad(jnp.take(table, mine, axis=0), jnp.take(accum, mine), share)
    all_rows, all_accum = (
        lax.all_gather(rows_next, "grp", axis=0, tiled=True),
        lax.all_gather(accum_next, "grp", axis=0, tiled=True),
    )
    new_table = table.at[listed].set(all_rows)
    new_accum = accum.at[listed].set(all_accum)
    return (new_table, new_accum)


def solution(mesh):
    return jax.shard_map(
        body,
        mesh=mesh,
        in_specs=(
            P("shard", None),
            P("shard"),
            P("grp", "shard", None, None),
            P("grp", "shard", None),
            P("grp", "shard", None),
            P("shard", None),
        ),
        out_specs=(P("shard", None), P("shard")),
        check_vma=False,
    )
```

profile of v0, /device:TPU:0, one launch (start us, length us, event | category | flops | bytes accessed | tf_op | source)
XLA Modules:
  0.0 196.8 jit_solution(4899026934540927414)
XLA Ops:
  7.2 0.8 copy.28
  7.9 4.5 %copy.27 = f32[4096,256]{1,0:T(8,128)} copy(f32[4096,256]{1,0:T(8,128)} %param.8) | data formatting | bytes 8388608
  12.5 2.3 %reduce-window.6 = s32[8,32,128]{2,1,0:T(8,128)S(1)} reduce-window(s32[8,32,128]{2,1,0:T(8,128)S(1)} %fusion.18, s32[]{:T(128)} %constant.94.clone.1), window={size=1x1x128 pad=0_0x0_0x127_0}, to_apply=%region_0.1 | reduce-window | flops 4161536 | bytes 262148 | tf_op jit(solution)/shard_map/reduce-window
  14.8 0.3 slice_reduce_fusion
  15.1 0.2 reduce-window.9
  15.3 0.1 add_bitcast_fusion
  15.4 0.1 fusion.17
  15.5 0.1 compare_select_fusion.1
  15.7 16.1 %scatter_custom_fusion = s32[4096]{0:T(1024)} fusion(s32[4096]{0:T(1024)S(1)} %bitcast.89, s32[4096]{0:T(1024)S(1)} %get-tuple-element.45, s32[]{:T(128)} %constant.102.clone.1), kind=kCustom, calls=%fused_computation.57 | custom fusion | bytes 16388 | tf_op jit(solution)/shard_map/scatter | solution.py:44
  31.7 7.3 %all-to-all-start = ((s32[8,1,512]{2,1,0:T(1,128)}), s32[8,1,512]{2,1,0:T(1,128)S(1)}, u32[]{:S(2)}, u32[]{:S(2)}) async-start(s32[8,1,512]{2,1,0:T(1,128)} %bitcast.14), calls=%async_computation | async-start | bytes 32768 | tf_op jit(solution)/shard_map/all_to_all | solution.py:49
  39.1 34.4 %scatter_custom_fusion.1 = bf16[4096,256]{1,0:T(8,128)(2,1)} fusion(s32[4096]{0:T(1024)S(1)} %bitcast.90, pred[4096]{0:T(1024)(128)(4,1)S(1)} %compare_and_fusion, bf16[]{:T(256)} %constant.108.clone.1, bf16[]{:T(256)} %constant.106.clone.1, bf16[512,256]{1,0:T(8,128)(2,1)S(1)} %bitcast.74, s32[4096]{0:T(1024)S(1)} %broadcast_clamp_fusion), kind=kCustom, calls=%fused_computation.15 | custom fusion | flops 1048576 | bytes 2379780 | tf_op jit(solution)/shard_map/scatter | solution.py:43
  73.5 6.1 %all-to-all-start.1 = ((bf16[8,512,256]{2,1,0:T(8,128)(2,1)}), bf16[8,512,256]{2,1,0:T(8,128)(2,1)S(1)}, u32[]{:S(2)}, u32[]{:S(2)}) async-start(bf16[8,512,256]{2,1,0:T(8,128)(2,1)} %bitcast.19), calls=%async_computation.1 | async-start | bytes 4194304 | tf_op jit(solution)/shard_map/all_to_all | solution.py:48
  79.7 47.6 %all-to-all-done.1 = bf16[8,512,256]{2,1,0:T(8,128)(2,1)S(1)} async-done(((bf16[8,512,256]{2,1,0:T(8,128)(2,1)}), bf16[8,512,256]{2,1,0:T(8,128)(2,1)S(1)}, u32[]{:S(2)}, u32[]{:S(2)}) %all-to-all-start.1) | async-done | bytes 2097184 | tf_op jit(solution)/shard_map/all_to_all | solution.py:48
  127.3 9.3 %while.10 = (s32[]{:T(128)}, f32[8,128,256]{2,1,0:T(8,128)}, s32[8,128]{1,0:T(8,128)S(1)}, s32[8,512]{1,0:T(8,128)S(1)}, bf16[4096,256]{1,0:T(8,128)(2,1)S(1)}, /*index=5*/s32[]{:T(128)}) while((s32[]{:T(128)}, f32[8,128,256]{2,1,0:T(8,128)}, s32[8,128]{1,0:T(8,128)S(1)}, s32[8,512]{1,0:T(8,128)S(1)}, bf16[4096,256]{1,0:T(8,128)(2,1)S(1)}, ...), condition=%wide.region_6.7_spmd, body=%wide.region_5.6_spmd.sunk | while | flops 268959744 | bytes 2278997 | solution.py:16
  127.3 1.1 fusion.34
  128.5 1.1 fusion.34
  129.6 1.1 fusion.34
  130.8 1.1 fusion.34
  131.9 1.1 fusion.34
  133.1 1.2 fusion.34
  134.3 1.1 fusion.34
  135.4 1.1 fusion.34
  136.6 0.0 all-gather.3.cloned.1.call-start
  136.7 1.7 gather_fusion.1
  138.4 3.2 %gather_fusion = f32[256,256]{1,0:T(8,128)S(1)} fusion(f32[4096,256]{1,0:T(8,128)} %copy.27, s32[1024]{0:T(1024)S(1)} %pad_clamp_fusion), kind=kCustom, calls=%fused_computation | custom fusion | bytes 525312 | tf_op jit(solution)/shard_map/jit(_take)/gather | solution.py:55
  141.6 19.1 %reduce-scatter.2.cloned.1.call-done = f32[256,256]{1,0:T(8,128)} async-done(((f32[1024,256]{1,0:T(8,128)}), f32[256,256]{1,0:T(8,128)}) %reduce-scatter.2.cloned.1.call-update) | async-done | bytes 262160 | tf_op jit(solution)/shard_map/reduce_scatter | solution.py:52
  160.7 1.1 multiply_reduce_fusion
  161.8 1.8 divide_subtract_fusion
  163.6 5.1 %all-gather = f32[4,1,256]{2,1,0:T(1,128)S(1)} all-gather(f32[1,1,256]{2,1,0:T(1,128)S(1)} %bitcast.95), channel_id=1, replica_groups=mesh['grp'=4,'shard'=8] {'grp'}, dimensions={0}, use_global_device_ids=true | all-gather | bytes 5120 | tf_op jit(solution)/shard_map/all_gather | solution.py:58
  168.7 4.3 %scatter_fusion.1 = f32[4096]{0:T(1024)S(1)} fusion(f32[4096]{0:T(1024)S(1)} %copy.28, s32[1024]{0:T(1024)S(1)} %bitcast.85, f32[1024]{0:T(1024)S(1)} %bitcast.87), kind=kCustom, calls=%fused_computation.6 | custom fusion | bytes 16384 | tf_op jit(solution)/shard_map/scatter | solution.py:61
  173.1 7.5 %all-gather.3.cloned.1.call-done = f32[1024,256]{1,0:T(8,128)} async-done(((f32[256,256]{1,0:T(8,128)}), f32[1024,256]{1,0:T(8,128)}) %all-gather.3.cloned.1.call-update) | async-done | bytes 1048592 | tf_op jit(solution)/shard_map/all_gather | solution.py:57
  180.5 9.4 %scatter_fusion = f32[4096,256]{1,0:T(8,128)} fusion(f32[4096,256]{1,0:T(8,128)} %copy.27, s32[1024]{0:T(1024)S(1)} %bitcast.86, f32[1024,256]{1,0:T(8,128)} %all-gather.3.cloned.1.call-done), kind=kCustom, calls=%fused_computation.5 | custom fusion | bytes 3149824 | tf_op jit(solution)/shard_map/scatter | solution.py:60
  (42 shorter events, 0.3 us)
Async XLA Ops:
  7.2 31.9 %copy-start = (bf16[1,1,512,256]{3,2,1,0:T(8,128)(2,1)S(1)}, bf16[1,1,512,256]{3,2,1,0:T(8,128)(2,1)}, u32[]{:S(2)}) copy-start(bf16[1,1,512,256]{3,2,1,0:T(8,128)(2,1)} %param.10) | copy-start | bytes 786436
  7.9 4.5 %copy-start.2 = (s32[1,1,4096]{2,1,0:T(1,128)S(1)}, s32[1,1,4096]{2,1,0:T(1,128)}, u32[]{:S(2)}) copy-start(s32[1,1,4096]{2,1,0:T(1,128)} %param.11) | copy-start | bytes 49156
  7.9 31.1 %copy-start.3 = (s32[1,1,4096]{2,1,0:T(1,128)S(1)}, s32[1,1,4096]{2,1,0:T(1,128)}, u32[]{:S(2)}) copy-start(s32[1,1,4096]{2,1,0:T(1,128)} %param.12) | copy-start | bytes 49156
  31.7 41.8 %all-to-all-start = ((s32[8,1,512]{2,1,0:T(1,128)}), s32[8,1,512]{2,1,0:T(1,128)S(1)}, u32[]{:S(2)}, u32[]{:S(2)}) async-start(s32[8,1,512]{2,1,0:T(1,128)} %bitcast.14), calls=%async_computation | async-start | bytes 32768 | tf_op jit(solution)/shard_map/all_to_all | solution.py:49
  73.5 53.8 %copy-start.4 = (s32[1,1024]{1,0:T(1,128)S(1)}, s32[1,1024]{1,0:T(1,128)}, u32[]{:S(2)}) copy-start(s32[1,1024]{1,0:T(1,128)} %param.13) | copy-start | bytes 12292
  73.5 53.8 %all-to-all-start.1 = ((bf16[8,512,256]{2,1,0:T(8,128)(2,1)}), bf16[8,512,256]{2,1,0:T(8,128)(2,1)S(1)}, u32[]{:S(2)}, u32[]{:S(2)}) async-start(bf16[8,512,256]{2,1,0:T(8,128)(2,1)} %bitcast.19), calls=%async_computation.1 | async-start | bytes 4194304 | tf_op jit(solution)/shard_map/all_to_all | solution.py:48
  79.6 81.1 %reduce-scatter.2.cloned.1.call-start = ((), (), s32[]{:S(2)}) async-start(), calls=%async_computation.3 | async-start | bytes 1310720 | tf_op jit(solution)/shard_map/reduce_scatter | solution.py:52
  136.6 43.9 %all-gather.3.cloned.1.call-start = ((), (), s32[]{:S(2)}) async-start(), calls=%async_computation.4 | async-start | bytes 1310720 | tf_op jit(solution)/shard_map/all_gather | solution.py:57
  173.0 16.9 %copy-start.1 = (f32[4096]{0:T(1024)}, f32[4096]{0:T(1024)S(1)}, u32[]{:S(2)}) copy-start(f32[4096]{0:T(1024)S(1)} %scatter_fusion.1) | copy-start | bytes 49156
Sparse Core Ops, SparseCore 0:
  136.7 23.9 reduce-scatter.1
  163.7 16.7 all-gather.2
where the time goes:
time: 197 us
  waiting for transfers between devices  74.3 us (38%)
  local copies, waits for them, and re-layouts  40.4 us (21%)
  other arithmetic  40.2 us (20%)
  between operations  14.2 us (7%)
  starting transfers between devices  13.5 us (7%)
  matrix products  9.15 us (5%)
  blocking collectives  5.07 us (3%)
    all_to_all x1, waiting for transfers between devices, body(): lax.all_to_all(send_grads, 'shard', split_axis=0, concat_axis=0, tiled=True)  47.6 us
    scatter x1, other arithmetic, body(): jnp.zeros((shards * slots_each, width), jnp.bfloat16).at[slot]  34.4 us
    reduce_scatter x1, waiting for transfers between devices, body(): share = lax.psum_scatter(grad_rows, 'grp', scatter_dimension=0, tiled=True)  19.1 us
    scatter x1, local copies, waits for them, and re-layouts, body(): jnp.full((shards * slots_each,), -1, jnp.int32).at[slot].set(ids % rows_dev)  16.1 us
    scatter x1, local copies, waits for them, and re-layouts, body(): new_table = table.at[listed].set(all_rows)  9.42 us
    dot_general x8, matrix products, one_block(): return jnp.dot(hits, slot_grads, preferred_element_type=jnp.float32)  9.15 us
    all_gather x1, waiting for transfers between devices, body(): lax.all_gather(rows_next, 'grp', axis=0, tiled=True)  7.46 us
    all_to_all x1, starting transfers between devices, body(): lax.all_to_all(send_rows, 'shard', split_axis=0, concat_axis=0, tiled=True)  7.25 us
  transfers between devices with their start and end apart: 4, of which 3 were waited for; matrix products, arithmetic and copies ran while one was open for 22% of the time, Pallas kernels for 0%

commit v1 on v0

v1 whole, which is shorter than its diff:
```python
import functools

import jax
import jax.numpy as jnp
from jax import lax
from jax.experimental import pallas as pl
from jax.experimental.pallas import tpu as pltpu
from jax.sharding import PartitionSpec as P

LANES = 128
MESH = pl.DeviceIdType.MESH
NT = (((1,), (1,)), ((), ()))


def log2(n):
    return n.bit_length() - 1


def grid_of(shards):
    x = 1
    while 4 * x * x <= shards:
        x *= 2
    return shards // x, x


def onehot(mask):
    return jnp.where(mask, 1.0, 0.0).astype(jnp.bfloat16)


def iota(shape, dim):
    return lax.broadcasted_iota(jnp.int32, shape, dim)


def route(ids_ref, bags_ref, shards, rows_dev, cap, left, right):
    lines = ids_ref.shape[0]
    ids, bags = ids_ref[...], bags_ref[...]
    owner = ids >> log2(rows_dev)
    local = ids & (rows_dev - 1)
    owned = [onehot(owner == s) for s in range(shards)]
    owned = jnp.concatenate(owned, axis=0)
    total = shards * lines
    before = onehot(iota((LANES, LANES), 0) < iota((LANES, LANES), 1))
    a, b = iota((total, total), 0), iota((total, total), 1)
    above = onehot(((a >> log2(lines)) == (b >> log2(lines))) & (b < a))
    counts = jnp.dot(above, owned, preferred_element_type=jnp.float32)
    offset = jnp.sum(counts, axis=1, keepdims=True)
    rank = jnp.dot(owned, before, preferred_element_type=jnp.float32) + offset
    slot = jnp.zeros((lines, LANES), jnp.float32)
    for s in range(shards):
        part = slice(s * lines, (s + 1) * lines)
        slot = slot + owned[part].astype(jnp.float32) * (rank[part] + float(s * cap))
    slot = slot.astype(jnp.int32)
    groups = shards * cap // LANES
    high, low = slot >> 7, slot & (LANES - 1)
    parts = [
        (local & 127).astype(jnp.float32),
        ((local >> 7) + 1).astype(jnp.float32),
        (bags & 127).astype(jnp.float32),
        (bags >> 7).astype(jnp.float32),
    ]
    group_no = iota((groups, LANES), 0)
    lane_no = iota((LANES, LANES), 0)
    for i in range(lines):
        at = slice(i * LANES, (i + 1) * LANES)
        hit = high[i : i + 1] == group_no
        for p, value in enumerate(parts):
            left[p * groups : (p + 1) * groups, at] = jnp.where(
                hit, value[i : i + 1], 0.0
            ).astype(jnp.bfloat16)
        right[:, at] = onehot(low[i : i + 1] == lane_no)
    placed = lax.dot_general(left[...], right[...], NT, preferred_element_type=jnp.float32)
    rows = (placed[groups : 2 * groups] - 1.0) * 128.0 + placed[:groups]
    samples = placed[3 * groups :] * 128.0 + placed[2 * groups : 3 * groups]
    return rows, samples


def share_kernel(
    shards, n_grp, rows_dev, cap, cut, chunks,
    g_ref, ids_ref, bags_ref, listed_ref, out_ref,
    blocks, tiles_out, tiles_in, left, right, listed_col, bag_hot, count, acc,
    sib_in, y_sums, final, sib_out,
    block_send, block_recv, tile_send, tile_recv, s1, r1, s2, r2, s3, r3,
):
    nz, nx = grid_of(shards)
    ny = n_grp // 2
    me = lax.axis_index("shard")
    grp = lax.axis_index("grp")
    z, x = me // nx, me % nx
    y, core = grp // 2, grp % 2
    samples, width = g_ref.shape
    touch = acc.shape[0]
    half = touch // 2
    piece = half // chunks
    other = (me + 1) % shards
    sibling = y * 2 + (1 - core)

    barrier = pltpu.get_barrier_semaphore()

    def greet_shard(o, c):
        pl.semaphore_signal(barrier, 1, device_id={"shard": (me + o) % shards}, device_id_type=MESH)
        return c

    def greet_grp(o, c):
        pl.semaphore_signal(barrier, 1, device_id={"grp": (grp + o) % n_grp}, device_id_type=MESH)
        return c

    lax.fori_loop(1, shards, greet_shard, 0)
    lax.fori_loop(1, n_grp, greet_grp, 0)
    blocks[me] = g_ref[...]
    pl.semaphore_wait(barrier, shards + n_grp - 2)

    spans = (pl.ds(0, cut), pl.ds(cut, samples - cut))

    def block_copy(part, src, way, to):
        where = blocks.at[src, spans[part]]
        return pltpu.make_async_remote_copy(
            src_ref=where,
            dst_ref=where,
            send_sem=block_send.at[part, src, way],
            recv_sem=block_recv.at[part, src],
            device_id={"shard": to},
            device_id_type=MESH,
        )

    def ways(part, zs, xs):
        on_z = (x == xs) if part == 0 else (z >= 0)
        on_x = (z == zs) if part == 1 else (x >= 0)
        return (
            (on_z & (z >= zs) & (z + 1 < nz), me + nx),
            (on_z & (z <= zs) & (z >= 1), me - nx),
            (on_x & (x >= xs) & (x + 1 < nx), me + 1),
            (on_x & (x <= xs) & (x >= 1), me - 1),
        )

    def forward(part, src, zs, xs):
        for way, (when, to) in enumerate(ways(part, zs, xs)):

            @pl.when(when)
            def _():
                block_copy(part, src, way, to).start()

    for part in (0, 1):
        forward(part, me, z, x)

    rows, bags = route(ids_ref, bags_ref, shards, rows_dev, cap, left, right)
    per = cap // LANES
    for s in range(shards):
        tiles_out[s, :per] = rows[s * per : (s + 1) * per]
        tiles_out[s, per:] = bags[s * per : (s + 1) * per]

    def tile_copy(dst):
        return pltpu.make_async_remote_copy(
            src_ref=tiles_out.at[dst],
            dst_ref=tiles_in.at[me],
            send_sem=tile_send.at[dst],
            recv_sem=tile_recv.at[me],
            device_id={"shard": dst},
            device_id_type=MESH,
        )

    def send_tile(o, c):
        tile_copy((me + o) % shards).start()
        return c

    lax.fori_loop(1, shards, send_tile, 0)
    tiles_in[me] = tiles_out[me]

    listed = listed_ref[...].astype(jnp.float32)
    for j in range(touch // LANES):
        listed_col[j * LANES : (j + 1) * LANES] = jnp.broadcast_to(
            listed[j : j + 1], (LANES, LANES)
        ).T
    acc[...] = jnp.zeros_like(acc)
    bag_no = iota((samples, LANES), 0).astype(jnp.float32)

    def one_source(src, zs, xs, own):
        @pl.when(jnp.logical_not(own))
        def _():
            pltpu.make_async_remote_copy(
                src_ref=tiles_out.at[src],
                dst_ref=tiles_in.at[src],
                send_sem=tile_send.at[src],
                recv_sem=tile_recv.at[src],
                device_id={"shard": other},
                device_id_type=MESH,
            ).wait_recv()

        tile = tiles_in[src]
        for c in range(per):
            bag_hot[:, c * LANES : (c + 1) * LANES] = onehot(bag_no == tile[per + c : per + c + 1])

        def build(k, carry):
            at = pl.ds(pl.multiple_of(k * LANES, LANES), LANES)
            col = listed_col[at]
            hits = [onehot(col == tile[c : c + 1]) for c in range(per)]
            found = lax.dot_general(
                jnp.concatenate(hits, axis=1), bag_hot[...], NT, preferred_element_type=jnp.float32
            )
            count[at] = found.astype(jnp.bfloat16)
            return carry

        lax.fori_loop(0, touch // LANES, build, 0)

        @pl.when(jnp.logical_not(own))
        def _():
            for part in (0, 1):
                block_copy(part, src, 0, other).wait_recv()
                forward(part, src, zs, xs)

        def add(k, carry):
            at = pl.ds(pl.multiple_of(k * LANES, LANES), LANES)
            acc[at] += jnp.dot(count[at], blocks[src], preferred_element_type=jnp.float32)
            return carry

        lax.fori_loop(0, touch // LANES, add, 0)

    def by_distance(i, carry):
        d = i // (2 * nx)
        xo = (i // 2) % nx
        zs = z + d * (1 - 2 * (i % 2))
        xs = (x + xo) % nx
        valid = (zs >= 0) & (zs < nz) & ((d > 0) | (i % 2 == 0))

        @pl.when(valid)
        def _():
            one_source(zs * nx + xs, zs, xs, (d == 0) & (xo == 0))

        return carry

    lax.fori_loop(0, 2 * nx * nz, by_distance, 0)

    def rows_at(base, c):
        return pl.ds(pl.multiple_of(base * half + c * piece, piece), piece)

    def first_copy(c):
        return pltpu.make_async_remote_copy(
            src_ref=acc.at[rows_at(1 - core, c)],
            dst_ref=sib_in.at[rows_at(0, c)],
            send_sem=s1.at[c],
            recv_sem=r1.at[c],
            device_id={"grp": sibling},
            device_id_type=MESH,
        )

    def y_copy(c, to_y, from_y):
        where = y_sums.at[from_y, rows_at(0, c)]
        return pltpu.make_async_remote_copy(
            src_ref=where,
            dst_ref=where,
            send_sem=s2.at[to_y, c],
            recv_sem=r2.at[from_y, c],
            device_id={"grp": to_y * 2 + core},
            device_id_type=MESH,
        )

    def last_copy(c):
        return pltpu.make_async_remote_copy(
            src_ref=final.at[rows_at(0, c)],
            dst_ref=sib_out.at[rows_at(0, c)],
            send_sem=s3.at[c],
            recv_sem=r3.at[c],
            device_id={"grp": sibling},
            device_id_type=MESH,
        )

    for c in range(chunks):
        first_copy(c).start()
    for c in range(chunks):
        first_copy(c).wait_recv()
        y_sums[y, rows_at(0, c)] = acc[rows_at(core, c)] + sib_in[rows_at(0, c)]
        for o in range(1, ny):
            y_copy(c, (y + o) % ny, y).start()
    for c in range(chunks):
        for o in range(1, ny):
            from_y = (y + o) % ny
            y_copy(c, from_y, from_y).wait_recv()
        total = y_sums[0, rows_at(0, c)]
        for k in range(1, ny):
            total = total + y_sums[k, rows_at(0, c)]
        final[rows_at(0, c)] = total
        last_copy(c).start()
        out_ref[rows_at(core, c)] = total
    for c in range(chunks):
        last_copy(c).wait_recv()
        out_ref[rows_at(1 - core, c)] = sib_out[rows_at(0, c)]

    for c in range(chunks):
        first_copy(c).wait_send()
        for o in range(1, ny):
            y_copy(c, (y + o) % ny, y).wait_send()
        last_copy(c).wait_send()

    def tile_sent(o, carry):
        tile_copy((me + o) % shards).wait_send()
        return carry

    lax.fori_loop(1, shards, tile_sent, 0)

    def block_sent(src, carry):
        for part in (0, 1):
            for way, (when, to) in enumerate(ways(part, src // nx, src % nx)):

                @pl.when(when)
                def _():
                    block_copy(part, src, way, to).wait_send()

        return carry

    lax.fori_loop(0, shards, block_sent, 0)


def summed(grads, ids, bags, listed, shards, n_grp, rows_dev):
    samples, width = grads.shape
    looks = ids.size
    touch = listed.size
    cap = looks // 8
    groups = shards * cap // LANES
    half = touch // 2
    chunks = 4
    cut = samples // 2
    f32, bf16 = jnp.float32, jnp.bfloat16
    vmem = pl.BlockSpec(memory_space=pltpu.VMEM)
    dma = pltpu.SemaphoreType.DMA
    return pl.pallas_call(
        functools.partial(share_kernel, shards, n_grp, rows_dev, cap, cut, chunks),
        out_shape=jax.ShapeDtypeStruct((touch, width), f32),
        in_specs=[vmem] * 4,
        out_specs=vmem,
        scratch_shapes=[
            pltpu.VMEM((shards, samples, width), bf16),
            pltpu.VMEM((shards, 2 * cap // LANES, LANES), f32),
            pltpu.VMEM((shards, 2 * cap // LANES, LANES), f32),
            pltpu.VMEM((4 * groups, looks), bf16),
            pltpu.VMEM((LANES, looks), bf16),
            pltpu.VMEM((touch, LANES), f32),
            pltpu.VMEM((samples, cap), bf16),
            pltpu.VMEM((touch, samples), bf16),
            pltpu.VMEM((touch, width), f32),
            pltpu.VMEM((half, width), f32),
            pltpu.VMEM((n_grp // 2, half, width), f32),
            pltpu.VMEM((half, width), f32),
            pltpu.VMEM((half, width), f32),
            dma((2, shards, 4)),
            dma((2, shards)),
            dma((shards,)),
            dma((shards,)),
            dma((chunks,)),
            dma((chunks,)),
            dma((n_grp // 2, chunks)),
            dma((n_grp // 2, chunks)),
            dma((chunks,)),
            dma((chunks,)),
        ],
        compiler_params=pltpu.CompilerParams(
            collective_id=0, has_side_effects=True, vmem_limit_bytes=48 * 2**20
        ),
    )(grads, ids, bags, listed)


def update_kernel(first_ref, table_ref, accum_ref, sums_ref, listed_ref, new_ref, new_accum_ref, halves):
    step = pl.program_id(0)
    width = table_ref.shape[1]
    blocks = table_ref.shape[0] // LANES

    @pl.when(step == 0)
    def _():
        sums = sums_ref[...]
        high = sums.astype(jnp.bfloat16)
        halves[:, :width] = high
        halves[:, width:] = (sums - high.astype(jnp.float32)).astype(jnp.bfloat16)

    for b in range(blocks):
        at = slice(b * LANES, (b + 1) * LANES)
        block = step * blocks + b
        first = first_ref[block]
        row_no = iota((LANES, LANES), 0) + block * LANES
        hot = [onehot(listed_ref[pl.ds(first + w, 1)] == row_no) for w in range(2)]
        found = jnp.dot(
            jnp.concatenate(hot, axis=1),
            halves[pl.ds(pl.multiple_of(first * LANES, LANES), 2 * LANES)],
            preferred_element_type=jnp.float32,
        )
        grads = found[:, :width] + found[:, width:]
        mean = jnp.sum(grads * grads, axis=1, keepdims=True) * (1.0 / width)
        accum = jnp.broadcast_to(accum_ref[b : b + 1], (LANES, LANES)).T
        accum_next = accum + mean
        scale = 0.5 / (jnp.sqrt(accum_next) + 1e-08)
        for w in range(width // LANES):
            cols = slice(w * LANES, (w + 1) * LANES)
            new_ref[at, cols] = table_ref[at, cols] - grads[:, cols] * scale
        new_accum_ref[b : b + 1] = accum_next.T[:1]


def update(table, accum, sums, listed, first):
    rows, width = table.shape
    touch = sums.shape[0]
    block = 1024
    lines = block // LANES
    return pl.pallas_call(
        update_kernel,
        grid_spec=pltpu.PrefetchScalarGridSpec(
            num_scalar_prefetch=1,
            grid=(rows // block,),
            in_specs=[
                pl.BlockSpec((block, width), lambda i, s: (i, 0)),
                pl.BlockSpec((lines, LANES), lambda i, s: (i, 0)),
                pl.BlockSpec((touch, width), lambda i, s: (0, 0)),
                pl.BlockSpec((touch // LANES, LANES), lambda i, s: (0, 0)),
            ],
            out_specs=[
                pl.BlockSpec((block, width), lambda i, s: (i, 0)),
                pl.BlockSpec((lines, LANES), lambda i, s: (i, 0)),
            ],
            scratch_shapes=[pltpu.VMEM((touch, 2 * width), jnp.bfloat16)],
        ),
        out_shape=[
            jax.ShapeDtypeStruct((rows, width), jnp.float32),
            jax.ShapeDtypeStruct((rows // LANES, LANES), jnp.float32),
        ],
        compiler_params=pltpu.CompilerParams(vmem_limit_bytes=32 * 2**20),
    )(first, table, accum, sums, listed)


def body(shards, n_grp, table, accum, pooled_grad, row_ids, bag_ids, touched):
    rows_dev, width = table.shape
    grads = pooled_grad.reshape(-1, width)
    ids = row_ids.reshape(-1, LANES)
    bags = bag_ids.reshape(-1, LANES)
    listed = touched.reshape(-1, LANES)
    sums = summed(grads, ids, bags, listed, shards, n_grp, rows_dev)
    starts = jnp.arange(rows_dev // LANES, dtype=jnp.int32) * LANES
    below = jnp.sum((touched.reshape(1, -1) < starts[:, None]).astype(jnp.int32), axis=1)
    first = jnp.minimum(below // LANES, listed.shape[0] - 2)
    new_table, new_accum = update(table, accum.reshape(-1, LANES), sums, listed, first)
    return new_table, new_accum.reshape(-1)


def solution(mesh):
    return jax.shard_map(
        functools.partial(body, mesh.shape["shard"], mesh.shape["grp"]),
        mesh=mesh,
        in_specs=(
            P("shard", None),
            P("shard"),
            P("grp", "shard", None, None),
            P("grp", "shard", None),
            P("grp", "shard", None),
            P("shard", None),
        ),
        out_specs=(P("shard", None), P("shard")),
        check_vma=False,
    )
```

time: 197 us -> 79 us (0.40)
  waiting for transfers between devices: 74.3 us -> 0 us
  Pallas kernels: 0 us -> 71 us
  other arithmetic: 40.2 us -> 0.89 us
  local copies, waits for them, and re-layouts: 40.4 us -> 5.97 us
  between operations: 14.2 us -> 0.67 us
  starting transfers between devices: 13.5 us -> 0 us
  matrix products: 9.15 us -> 0 us
  blocking collectives: 5.07 us -> 0 us
    pallas_call x0 -> x2, Pallas kernels: none -> 71 us  [the longest x1 65.9 us: summed(): pl.pallas_call(functools.partial(share_kernel, shards, n_grp, rows_dev, c...]
    all_to_all x2 -> x0, waiting for transfers between devices: 47.6 us -> none  [the longest x1 47.6 us: body(): lax.all_to_all(send_grads, 'shard', split_axis=0, concat_axis=0, tiled=True)]
    scatter x1 -> x0, other arithmetic: 34.4 us -> none  [body(): jnp.zeros((shards * slots_each, width), jnp.bfloat16).at[slot]]
    scatter x3 -> x0, local copies, waits for them, and re-layouts: 29.8 us -> none  [the longest x1 16.1 us: body(): jnp.full((shards * slots_each,), -1, jnp.int32).at[slot].set(ids % rows_dev)]
    reduce_scatter x1 -> x0, waiting for transfers between devices: 19.1 us -> none  [body(): share = lax.psum_scatter(grad_rows, 'grp', scatter_dimension=0, tiled=True)]
    all_to_all x2 -> x0, starting transfers between devices: 13.4 us -> none  [the longest x1 7.25 us: body(): lax.all_to_all(send_rows, 'shard', split_axis=0, concat_axis=0, tiled=True)]
    dot_general x8 -> x0, matrix products: 9.15 us -> none  [one_block(): return jnp.dot(hits, slot_grads, preferred_element_type=jnp.float32)]
    all_gather x1 -> x0, waiting for transfers between devices: 7.46 us -> none  [body(): lax.all_gather(rows_next, 'grp', axis=0, tiled=True)]
  transfers between devices with their start and end apart: 4 -> 0, of which waited for: 3 -> 0; matrix products, arithmetic and copies ran while one was open for 22% -> 0% of each run, Pallas kernels for 0% -> 0%
where the time goes in v1:
time: 79 us; the launch traced here: 78.5 us
  Pallas kernels  71 us (90%)
  local copies, waits for them, and re-layouts  5.97 us (8%)
  other arithmetic  0.89 us (1%)
    pallas_call x1, Pallas kernels, summed(): pl.pallas_call(functools.partial(share_kernel, shards, n_grp, rows_dev, c...  65.9 us
    unnamed x12, local copies, waits for them, and re-layouts  5.97 us
    pallas_call x1, Pallas kernels, update(): pl.pallas_call(update_kernel, grid_spec=pltpu.PrefetchScalarGridSpec(num_...  5.05 us

profile of v1, /device:TPU:0, one launch (start us, length us, event | category | flops | bytes accessed | tf_op | source)
XLA Modules:
  0.0 78.5 jit_solution(3463792002074973656)
XLA Ops:
  0.6 0.9 %convert_reduce_fusion = s32[32]{0:T(128)S(1)} fusion(s32[1024]{0:T(1024)} %bitcast.8, s32[32]{0:T(128)S(1)} %iota_multiply_fusion), kind=kLoop, calls=%fused_computation | loop fusion | flops 98272 | bytes 4352 | tf_op jit(solution)/shard_map/reduce_sum | solution.py:432
  1.5 0.0 copy-start.1
  1.5 0.9 %copy-done.1 = bf16[1,1,512,256]{3,2,1,0:T(8,128)(2,1)S(1)} copy-done((bf16[1,1,512,256]{3,2,1,0:T(8,128)(2,1)S(1)}, bf16[1,1,512,256]{3,2,1,0:T(8,128)(2,1)}, u32[]{:S(2)}) %copy-start.1) | copy-done | bytes 262168
  2.5 0.0 copy-start.2
  2.5 0.7 copy-done.2
  3.2 0.0 copy-start.3
  3.2 0.7 copy-done.3
  3.9 0.0 copy-start.4
  3.9 0.7 copy-done.4
  4.6 65.9 %shard_map.77.sums_ref = f32[1024,256]{1,0:T(8,128)S(1)} custom-call(bf16[512,256]{1,0:T(8,128)(2,1)S(1)} %bitcast.7, s32[32,128]{1,0:T(8,128)S(1)} %bitcast.11, s32[32,128]{1,0:T(8,128)S(1)} %bitcast.12, s32[8,128]{1,0:T(8,128)S(1)} %bitcast.9), custom_call_target="tpu_custom_call" | custom-call | tf_op jit(solution)/shard_map/pallas_call | solution.py:324
  70.6 0.0 copy-start
  70.6 2.2 %copy-done = f32[4096,256]{1,0:T(8,128)S(1)} copy-done((f32[4096,256]{1,0:T(8,128)S(1)}, f32[4096,256]{1,0:T(8,128)}, u32[]{:S(2)}) %copy-start) | copy-done | bytes 4194328
  72.8 0.0 copy-start.5
  72.8 0.7 copy-done.5
  73.5 5.0 %shard_map.78 = (f32[4096,256]{1,0:T(8,128)}, f32[32,128]{1,0:T(8,128)}) custom-call(s32[32]{0:T(128)S(1)} %fusion.first_ref, f32[4096,256]{1,0:T(8,128)S(1)} %copy-done, f32[32,128]{1,0:T(8,128)S(1)} %bitcast.13, f32[1024,256]{1,0:T(8,128)S(1)} %shard_map.77.sums_ref, s32[8,128]{1,0:T(8,128)S(1)} %bitcast.10), custom_call_target="tpu_custom_call" | custom-call | tf_op jit(solution)/shard_map/pallas_call | solution.py:399
  (2 shorter events, 0.0 us)
Async XLA Ops:
  1.5 1.0 %copy-start.1 = (bf16[1,1,512,256]{3,2,1,0:T(8,128)(2,1)S(1)}, bf16[1,1,512,256]{3,2,1,0:T(8,128)(2,1)}, u32[]{:S(2)}) copy-start(bf16[1,1,512,256]{3,2,1,0:T(8,128)(2,1)} %param.8) | copy-start | bytes 786436
  2.5 0.7 copy-start.2
  3.2 0.7 copy-start.3
  3.9 0.7 copy-start.4
  70.6 2.2 %copy-start = (f32[4096,256]{1,0:T(8,128)S(1)}, f32[4096,256]{1,0:T(8,128)}, u32[]{:S(2)}) copy-start(f32[4096,256]{1,0:T(8,128)} %table_ref.1) | copy-start | bytes 12582916
  72.8 0.7 copy-start.5

commit v2 on v1

--- a/solution.py
+++ b/solution.py
@@ -75,11 +75,12 @@
 
 
 def share_kernel(
-    shards, n_grp, rows_dev, cap, cut, chunks,
-    g_ref, ids_ref, bags_ref, listed_ref, out_ref,
-    blocks, tiles_out, tiles_in, left, right, listed_col, bag_hot, count, acc,
+    shards, n_grp, rows_dev, cap, cuts, chunks,
+    g_hbm, ids_hbm, bags_hbm, listed_hbm, out_ref,
+    ids_ref, bags_ref, listed_ref,
+    blocks, tiles_out, tiles_in, left, right, listed_col, bag_hot, row_hot, picked, acc,
     sib_in, y_sums, final, sib_out,
-    block_send, block_recv, tile_send, tile_recv, s1, r1, s2, r2, s3, r3,
+    load_sem, block_send, block_recv, tile_send, tile_recv, s1, r1, s2, r2, s3, r3,
 ):
     nz, nx = grid_of(shards)
     ny = n_grp // 2
@@ -87,13 +88,27 @@
     grp = lax.axis_index("grp")
     z, x = me // nx, me % nx
     y, core = grp // 2, grp % 2
-    samples, width = g_ref.shape
+    samples, width = g_hbm.shape
     touch = acc.shape[0]
     half = touch // 2
     piece = half // chunks
     other = (me + 1) % shards
     sibling = y * 2 + (1 - core)
 
+    loads = [
+        pltpu.make_async_copy(src, dst, load_sem.at[i])
+        for i, (src, dst) in enumerate(
+            [
+                (g_hbm, blocks.at[me]),
+                (ids_hbm, ids_ref),
+                (bags_hbm, bags_ref),
+                (listed_hbm, listed_ref),
+            ]
+        )
+    ]
+    for load in loads:
+        load.start()
+
     barrier = pltpu.get_barrier_semaphore()
 
     def greet_shard(o, c):
@@ -106,10 +121,12 @@
 
     lax.fori_loop(1, shards, greet_shard, 0)
     lax.fori_loop(1, n_grp, greet_grp, 0)
-    blocks[me] = g_ref[...]
     pl.semaphore_wait(barrier, shards + n_grp - 2)
-
-    spans = (pl.ds(0, cut), pl.ds(cut, samples - cut))
+    loads[0].wait()
+
+    edges = (0, *cuts, samples)
+    spans = [pl.ds(a, b - a) for a, b in zip(edges, edges[1:])]
+    parts = range(len(spans))
 
     def block_copy(part, src, way, to):
         where = blocks.at[src, spans[part]]
@@ -123,8 +140,8 @@
         )
 
     def ways(part, zs, xs):
-        on_z = (x == xs) if part == 0 else (z >= 0)
-        on_x = (z == zs) if part == 1 else (x >= 0)
+        on_z = (x == xs) if part % 2 == 0 else (z >= 0)
+        on_x = (z == zs) if part % 2 == 1 else (x >= 0)
         return (
             (on_z & (z >= zs) & (z + 1 < nz), me + nx),
             (on_z & (z <= zs) & (z >= 1), me - nx),
@@ -139,9 +156,11 @@
             def _():
                 block_copy(part, src, way, to).start()
 
-    for part in (0, 1):
+    for part in parts:
         forward(part, me, z, x)
 
+    for load in loads[1:]:
+        load.wait()
     rows, bags = route(ids_ref, bags_ref, shards, rows_dev, cap, left, right)
     per = cap // LANES
     for s in range(shards):
@@ -171,7 +190,8 @@
             listed[j : j + 1], (LANES, LANES)
         ).T
     acc[...] = jnp.zeros_like(acc)
-    bag_no = iota((samples, LANES), 0).astype(jnp.float32)
+    bag_no = iota((LANES, samples), 1).astype(jnp.float32)
+    half_rows = touch // 2
 
     def one_source(src, zs, xs, own):
         @pl.when(jnp.logical_not(own))
@@ -187,32 +207,30 @@
 
         tile = tiles_in[src]
         for c in range(per):
-            bag_hot[:, c * LANES : (c + 1) * LANES] = onehot(bag_no == tile[per + c : per + c + 1])
+            column = jnp.broadcast_to(tile[per + c : per + c + 1], (LANES, LANES)).T
+            bag_hot[c * LANES : (c + 1) * LANES] = onehot(bag_no == column[:, :1])
 
         def build(k, carry):
             at = pl.ds(pl.multiple_of(k * LANES, LANES), LANES)
             col = listed_col[at]
-            hits = [onehot(col == tile[c : c + 1]) for c in range(per)]
-            found = lax.dot_general(
-                jnp.concatenate(hits, axis=1), bag_hot[...], NT, preferred_element_type=jnp.float32
-            )
-            count[at] = found.astype(jnp.bfloat16)
+            for c in range(per):
+                row_hot[at, c * LANES : (c + 1) * LANES] = onehot(col == tile[c : c + 1])
             return carry
 
         lax.fori_loop(0, touch // LANES, build, 0)
 
         @pl.when(jnp.logical_not(own))
         def _():
-            for part in (0, 1):
+            for part in parts:
                 block_copy(part, src, 0, other).wait_recv()
                 forward(part, src, zs, xs)
 
-        def add(k, carry):
-            at = pl.ds(pl.multiple_of(k * LANES, LANES), LANES)
-            acc[at] += jnp.dot(count[at], blocks[src], preferred_element_type=jnp.float32)
-            return carry
-
-        lax.fori_loop(0, touch // LANES, add, 0)
+        picked[...] = jnp.dot(
+            bag_hot[...], blocks[src], preferred_element_type=jnp.float32
+        ).astype(jnp.bfloat16)
+        for h in range(2):
+            at = slice(h * half_rows, (h + 1) * half_rows)
+            acc[at] += jnp.dot(row_hot[at], picked[...], preferred_element_type=jnp.float32)
 
     def by_distance(i, carry):
         d = i // (2 * nx)
@@ -297,7 +315,7 @@
     lax.fori_loop(1, shards, tile_sent, 0)
 
     def block_sent(src, carry):
-        for part in (0, 1):
+        for part in parts:
             for way, (when, to) in enumerate(ways(part, src // nx, src % nx)):
 
                 @pl.when(when)
@@ -317,31 +335,36 @@
     groups = shards * cap // LANES
     half = touch // 2
     chunks = 4
-    cut = samples // 2
+    cuts = (samples * 5 // 16, samples // 2, samples * 25 // 32)
     f32, bf16 = jnp.float32, jnp.bfloat16
     vmem = pl.BlockSpec(memory_space=pltpu.VMEM)
     dma = pltpu.SemaphoreType.DMA
     return pl.pallas_call(
-        functools.partial(share_kernel, shards, n_grp, rows_dev, cap, cut, chunks),
+        functools.partial(share_kernel, shards, n_grp, rows_dev, cap, cuts, chunks),
         out_shape=jax.ShapeDtypeStruct((touch, width), f32),
-        in_specs=[vmem] * 4,
+        in_specs=[pl.BlockSpec(memory_space=pl.ANY)] * 4,
         out_specs=vmem,
         scratch_shapes=[
+            pltpu.VMEM(ids.shape, jnp.int32),
+            pltpu.VMEM(bags.shape, jnp.int32),
+            pltpu.VMEM(listed.shape, jnp.int32),
             pltpu.VMEM((shards, samples, width), bf16),
             pltpu.VMEM((shards, 2 * cap // LANES, LANES), f32),
             pltpu.VMEM((shards, 2 * cap // LANES, LANES), f32),
             pltpu.VMEM((4 * groups, looks), bf16),
             pltpu.VMEM((LANES, looks), bf16),
             pltpu.VMEM((touch, LANES), f32),
-            pltpu.VMEM((samples, cap), bf16),
-            pltpu.VMEM((touch, samples), bf16),
+            pltpu.VMEM((cap, samples), bf16),
+            pltpu.VMEM((touch, cap), bf16),
+            pltpu.VMEM((cap, width), bf16),
             pltpu.VMEM((touch, width), f32),
             pltpu.VMEM((half, width), f32),
             pltpu.VMEM((n_grp // 2, half, width), f32),
             pltpu.VMEM((half, width), f32),
             pltpu.VMEM((half, width), f32),
-            dma((2, shards, 4)),
-            dma((2, shards)),
+            dma((4,)),
+            dma((len(cuts) + 1, shards, 4)),
+            dma((len(cuts) + 1, shards)),
             dma((shards,)),
             dma((shards,)),
             dma((chunks,)),
@@ -352,12 +375,12 @@
             dma((chunks,)),
         ],
         compiler_params=pltpu.CompilerParams(
-            collective_id=0, has_side_effects=True, vmem_limit_bytes=48 * 2**20
+            collective_id=0, has_side_effects=True, vmem_limit_bytes=60 * 2**20
         ),
     )(grads, ids, bags, listed)
 
 
-def update_kernel(first_ref, table_ref, accum_ref, sums_ref, listed_ref, new_ref, new_accum_ref, halves):
+def update_kernel(table_ref, accum_ref, sums_ref, listed_ref, new_ref, new_accum_ref, halves):
     step = pl.program_id(0)
     width = table_ref.shape[1]
     blocks = table_ref.shape[0] // LANES
@@ -372,7 +395,8 @@
     for b in range(blocks):
         at = slice(b * LANES, (b + 1) * LANES)
         block = step * blocks + b
-        first = first_ref[block]
+        below = jnp.sum(jnp.where(listed_ref[...] < block * LANES, 1.0, 0.0)).astype(jnp.int32)
+        first = jnp.minimum(below >> 7, listed_ref.shape[0] - 2)
         row_no = iota((LANES, LANES), 0) + block * LANES
         hot = [onehot(listed_ref[pl.ds(first + w, 1)] == row_no) for w in range(2)]
         found = jnp.dot(
@@ -391,25 +415,24 @@
         new_accum_ref[b : b + 1] = accum_next.T[:1]
 
 
-def update(table, accum, sums, listed, first):
+def update(table, accum, sums, listed):
     rows, width = table.shape
     touch = sums.shape[0]
     block = 1024
     lines = block // LANES
     return pl.pallas_call(
         update_kernel,
-        grid_spec=pltpu.PrefetchScalarGridSpec(
-            num_scalar_prefetch=1,
+        grid_spec=pl.GridSpec(
             grid=(rows // block,),
             in_specs=[
-                pl.BlockSpec((block, width), lambda i, s: (i, 0)),
-                pl.BlockSpec((lines, LANES), lambda i, s: (i, 0)),
-                pl.BlockSpec((touch, width), lambda i, s: (0, 0)),
-                pl.BlockSpec((touch // LANES, LANES), lambda i, s: (0, 0)),
+                pl.BlockSpec((block, width), lambda i: (i, 0)),
+                pl.BlockSpec((lines, LANES), lambda i: (i, 0)),
+                pl.BlockSpec((touch, width), lambda i: (0, 0)),
+                pl.BlockSpec((touch // LANES, LANES), lambda i: (0, 0)),
             ],
             out_specs=[
-                pl.BlockSpec((block, width), lambda i, s: (i, 0)),
-                pl.BlockSpec((lines, LANES), lambda i, s: (i, 0)),
+                pl.BlockSpec((block, width), lambda i: (i, 0)),
+                pl.BlockSpec((lines, LANES), lambda i: (i, 0)),
             ],
             scratch_shapes=[pltpu.VMEM((touch, 2 * width), jnp.bfloat16)],
         ),
@@ -417,8 +440,8 @@
             jax.ShapeDtypeStruct((rows, width), jnp.float32),
             jax.ShapeDtypeStruct((rows // LANES, LANES), jnp.float32),
         ],
-        compiler_params=pltpu.CompilerParams(vmem_limit_bytes=32 * 2**20),
-    )(first, table, accum, sums, listed)
+        compiler_params=pltpu.CompilerParams(vmem_limit_bytes=60 * 2**20),
+    )(table, accum, sums, listed)
 
 
 def body(shards, n_grp, table, accum, pooled_grad, row_ids, bag_ids, touched):
@@ -428,10 +451,7 @@
     bags = bag_ids.reshape(-1, LANES)
     listed = touched.reshape(-1, LANES)
     sums = summed(grads, ids, bags, listed, shards, n_grp, rows_dev)
-    starts = jnp.arange(rows_dev // LANES, dtype=jnp.int32) * LANES
-    below = jnp.sum((touched.reshape(1, -1) < starts[:, None]).astype(jnp.int32), axis=1)
-    first = jnp.minimum(below // LANES, listed.shape[0] - 2)
-    new_table, new_accum = update(table, accum.reshape(-1, LANES), sums, listed, first)
+    new_table, new_accum = update(table, accum.reshape(-1, LANES), sums, listed)
     return new_table, new_accum.reshape(-1)
 
 

time: 79 us -> 60.9 us (0.77)
  Pallas kernels: 71 us -> 60.1 us
  local copies, waits for them, and re-layouts: 5.97 us -> 0 us
  other arithmetic: 0.89 us -> 0 us
    pallas_call x1, Pallas kernels: 65.9 us -> 52.7 us  [summed(): pl.pallas_call(functools.partial(share_kernel, shards, n_grp, rows_dev, c...]
    unnamed x12 -> x0, local copies, waits for them, and re-layouts: 5.97 us -> none
    pallas_call x1, Pallas kernels: 5.05 us -> 7.37 us  [update(): pl.pallas_call(update_kernel, grid_spec=pl.GridSpec(grid=(rows // block,)...]
    reduce_sum x1 -> x0, other arithmetic: 0.88 us -> none  [body(): jnp.sum((touched.reshape(1, -1) < starts[:, None]).astype(jnp.int32), axi...]
where the time goes in v2:
time: 60.9 us; the launch traced here: 60.7 us
  Pallas kernels  60.1 us (99%)
  between operations  0.64 us (1%)
    pallas_call x1, Pallas kernels, summed(): pl.pallas_call(functools.partial(share_kernel, shards, n_grp, rows_dev, c...  52.7 us
    pallas_call x1, Pallas kernels, update(): pl.pallas_call(update_kernel, grid_spec=pl.GridSpec(grid=(rows // block,)...  7.37 us

profile of v2, /device:TPU:0, one launch (start us, length us, event | category | flops | bytes accessed | tf_op | source)
XLA Modules:
  0.0 60.7 jit_solution(9635260941311211845)
XLA Ops:
  0.6 52.7 %shard_map.77.sums_ref = f32[1024,256]{1,0:T(8,128)} custom-call(bf16[512,256]{1,0:T(8,128)(2,1)} %bitcast.6, s32[32,128]{1,0:T(8,128)} %bitcast.7, s32[32,128]{1,0:T(8,128)} %bitcast.8, s32[8,128]{1,0:T(8,128)} %bitcast.10), custom_call_target="tpu_custom_call" | custom-call | tf_op jit(solution)/shard_map/pallas_call | solution.py:342
  53.4 7.4 %shard_map.78 = (f32[4096,256]{1,0:T(8,128)}, f32[32,128]{1,0:T(8,128)}) custom-call(f32[4096,256]{1,0:T(8,128)} %table_ref.1, f32[32,128]{1,0:T(8,128)} %bitcast.9, f32[1024,256]{1,0:T(8,128)} %shard_map.77.sums_ref, s32[8,128]{1,0:T(8,128)} %bitcast.11), custom_call_target="tpu_custom_call" | custom-call | tf_op jit(solution)/shard_map/pallas_call | solution.py:423
